TPU v7x, 32 devices: a whole 2x2x4 slice. The times are simulated.
32 devices in a mesh: parts: 2 (over y), seq: 4 (over z), mp: 2 (over x), batch: 2 (over core).
Axes of the slice: x: 2, y: 2, z: 4, core: 2. Of those that a mesh axis runs over, the one named last changes fastest.
Arguments:
- hidden_acts: bfloat16 [4, 4096, 14336], P(('parts', 'batch'), 'seq', 'mp'), parts along dimension 0, may hold values from -6 to 6
- out_cotangent: bfloat16 [4, 4096, 4096], P(('parts', 'batch'), 'seq', 'mp'), parts along dimension 0, may hold values from -6 to 6
- in_projection: bfloat16 [14336, 64], P('mp'), may hold values from -0.046875 to 0.046875
- out_projection: bfloat16 [4096, 64], P('mp'), may hold values from -0.09375 to 0.09375
- step_lengths: int32 [4, 128], P(('parts', 'batch')), parts along dimension 0, may hold values from 1 to 2048, 4096 in all within a row
- query_grads: bfloat16 [256, 4096], P('seq', 'mp'), may hold values from -0.01171875 to 0.01171875
- query_trace: int32 [256], replicated, may hold values from 0 to 1
Outputs:
- scores: float32 [4, 128, 256], P(('parts', 'batch'), 'seq'), parts along dimension 0
There are 2 independent parts, one for each index of `parts`. A program takes and returns all parts, laid end to end along the dimension named above; an argument that names none is the same for every part. Nothing has to cross between parts.
Inputs may be any that keep to these rules, and one draw needn't show every extreme that they name: `step_lengths`: the 128 lengths of each trace add up to 4096, and the longest is 2048.
All inputs are finite; a program needn't handle non-finite values.
Results may differ from a plain program's by a relative error of at most 0.0051.
Values may be sent and summed in bfloat16 or wider, within the bound.
A program may use at most 64 MiB of HBM per device.

v0:
```python
import jax
import jax.numpy as jnp
from jax import lax
from jax.sharding import PartitionSpec as P


def rows_times(left, right):
    return lax.dot_general(
        left, right, (((1,), (1,)), ((), ())), preferred_element_type=jnp.float32
    )


def masked_product(first_pos, end_pos, positions, out_rows, in_rows):
    member = (positions[None, :] >= first_pos[:, None]) & (positions[None, :] < end_pos[:, None])
    weighted = jnp.where(member[:, None, :], out_rows[None, :, :], jnp.zeros((), jnp.bfloat16))
    step_count = first_pos.shape[0]
    share_rows = out_rows.shape[0]
    gradients = jnp.dot(
        weighted.reshape(step_count * share_rows, positions.shape[0]),
        in_rows,
        preferred_element_type=jnp.float32,
    )
    return gradients.reshape(step_count, share_rows * in_rows.shape[1])


def per_device(
    hidden_acts,
    out_cotangent,
    in_projection,
    out_projection,
    step_lengths,
    query_grads,
    query_trace,
):
    activations = hidden_acts[0]
    cotangent = out_cotangent[0]
    lengths = step_lengths[0]
    in_part = jnp.dot(activations, in_projection, preferred_element_type=jnp.float32)
    out_part = jnp.dot(cotangent, out_projection, preferred_element_type=jnp.float32)
    in_total = lax.psum(in_part, "mp")
    out_mine = lax.psum_scatter(out_part, "mp", scatter_dimension=1, tiled=True)
    in_low = in_total.astype(jnp.bfloat16)
    out_low = out_mine.astype(jnp.bfloat16)
    token_count = activations.shape[0]
    step_ends = jnp.cumsum(lengths, dtype=jnp.int32)
    step_starts = step_ends - lengths
    positions = lax.axis_index("seq") * token_count + jnp.arange(token_count, dtype=jnp.int32)
    out_rows = out_low.T
    step_grads = lax.psum_scatter(
        masked_product(step_starts, step_ends, positions, out_rows, in_low),
        "seq",
        scatter_dimension=0,
        tiled=True,
    )
    step_low = step_grads.astype(jnp.bfloat16)
    trace_index = lax.axis_index("batch")
    gathered = lax.all_gather(query_grads, "seq", axis=0, tiled=True)
    partial_value = rows_times(step_low, gathered)
    totals = lax.psum(partial_value, "mp")
    result = jnp.where(query_trace[None, :] != trace_index, totals, jnp.zeros((), jnp.float32))
    return result[None]


def solution(mesh):
    return jax.shard_map(
        per_device,
        mesh=mesh,
        in_specs=(
            P(("parts", "batch"), "seq", "mp"),
            P(("parts", "batch"), "seq", "mp"),
            P("mp", None),
            P("mp", None),
            P(("parts", "batch"), None),
            P("seq", "mp"),
            P(),
        ),
        out_specs=P(("parts", "batch"), "seq", None),
        check_vma=False,
    )
```

profile of v0, /device:TPU:0, one launch (start us, length us, event | category | flops | bytes accessed | tf_op | source)
XLA Modules:
  0.0 91.8 jit_solution(12966277191605111953)
XLA Ops:
  7.4 0.0 copy-start
  7.4 0.0 reduce-scatter.3.cloned.1.call-start
  7.4 4.4 %fusion.2 = f32[1024,64]{0,1:T(8,128)} fusion(bf16[2048,64]{0,1:T(8,128)(2,1)} %param.10, bf16[1,1024,2048]{2,1,0:T(8,128)(2,1)} %param.8), kind=kOutput, calls=%fused_computation.3 | convolution fusion | flops 268435456 | bytes 4718592 | tf_op jit(solution)/shard_map/dot_general | solution.py:39
  11.8 0.0 reduce-scatter.3.cloned.1.call-update
  11.8 0.0 all-gather.2.cloned.1.call-start
  11.9 0.5 all-gather.2.cloned.1.call-update
  12.4 0.0 reduce-scatter.5.cloned.1.call-start
  12.4 0.8 copy.9
  13.2 0.2 reduce-window.7
  13.4 0.1 reduce
  13.5 0.7 bitcast_subtract_fusion
  14.1 0.0 copy-done
  14.1 7.2 %fusion = f32[1024,64]{1,0:T(8,128)S(1)} fusion(bf16[7168,64]{0,1:T(8,128)(2,1)S(1)} %copy-done, bf16[1,1024,7168]{2,1,0:T(8,128)(2,1)} %param.7), kind=kOutput, calls=%fused_computation | convolution fusion | flops 939524096 | bytes 15859712 | tf_op jit(solution)/shard_map/dot_general | solution.py:38
  21.4 18.7 %all-reduce.1 = bf16[1024,64]{1,0:T(8,128)(2,1)S(1)} all-reduce(f32[1024,64]{1,0:T(8,128)S(1)} %fusion), channel_id=1, replica_groups=mesh['parts'=2,'seq'=4,'mp'=2,'batch'=2] {'mp'}, use_global_device_ids=true, to_apply=%region_2.0 | all-reduce | flops 65536 | bytes 393216 | tf_op jit(solution)/shard_map/psum | solution.py:40
  40.1 0.2 compare_and_fusion
  40.2 0.0 reduce-scatter.3.cloned.1.call-done
  40.3 0.9 convert_bitcast_fusion
  41.2 0.7 broadcast_select_fusion
  41.9 0.0 copy-start.1
  42.0 2.4 %fusion.8 = f32[4096,64]{1,0:T(8,128)S(1)} fusion(bf16[4096,1024]{1,0:T(8,128)(2,1)S(1)} %bitcast.19, bf16[1024,64]{1,0:T(8,128)(2,1)S(1)} %all-reduce.1), kind=kOutput, calls=%fused_computation.15 | convolution fusion | flops 536870912 | bytes 9568256 | tf_op jit(solution)/shard_map/dot_general | solution.py:18
  44.3 1.7 %reshape.93 = f32[128,2048]{1,0:T(8,128)} reshape(f32[4096,64]{1,0:T(8,128)S(1)} %fusion.8) | data formatting | bytes 2097152 | tf_op jit(solution)/shard_map/reshape | solution.py:23
  46.0 0.0 reduce-scatter.5.cloned.1.call-update
  46.1 0.0 copy-done.1
  46.1 0.0 all-gather.2.cloned.1.call-done
  46.1 27.5 %reduce-scatter.5.cloned.1.call-done = f32[32,2048]{1,0:T(8,128)} async-done(((f32[128,2048]{1,0:T(8,128)}), f32[32,2048]{1,0:T(8,128)}) %reduce-scatter.5.cloned.1.call-update) | async-done | bytes 262160 | tf_op jit(solution)/shard_map/reduce_scatter | solution.py:49
  73.6 1.7 %fusion.6 = f32[32,256]{1,0:T(8,128)S(1)} fusion(bf16[256,2048]{1,0:T(8,128)(2,1)} %all-gather.2.cloned.1.call-done, f32[32,2048]{1,0:T(8,128)} %reduce-scatter.5.cloned.1.call-done), kind=kOutput, calls=%fused_computation.8 | convolution fusion | flops 33619968 | bytes 1343488 | tf_op jit(solution)/shard_map/dot_general | solution.py:8
  75.4 8.4 %psum.15 = f32[32,256]{1,0:T(8,128)S(1)} all-reduce(f32[32,256]{1,0:T(8,128)S(1)} %fusion.6), channel_id=1, replica_groups=mesh['parts'=2,'seq'=4,'mp'=2,'batch'=2] {'mp'}, use_global_device_ids=true, to_apply=%region_4.5 | all-reduce | flops 8192 | bytes 65536 | tf_op jit(solution)/shard_map/psum | solution.py:59
  83.8 0.6 select_bitcast_fusion
  (2 shorter events, 0.0 us)
Async XLA Ops:
  7.4 6.8 %copy-start = (bf16[7168,64]{0,1:T(8,128)(2,1)S(1)}, bf16[7168,64]{0,1:T(8,128)(2,1)}, u32[]{:S(2)}) copy-start(bf16[7168,64]{0,1:T(8,128)(2,1)} %param.9) | copy-start | bytes 2752516
  7.4 32.9 %reduce-scatter.3.cloned.1.call-start = ((), (), s32[]{:S(2)}) async-start(), calls=%async_computation.2 | async-start | bytes 393216 | tf_op jit(solution)/shard_map/reduce_scatter | solution.py:41
  11.8 34.3 %all-gather.2.cloned.1.call-start = ((), (), s32[]{:S(2)}) async-start(), calls=%async_computation.4 | async-start | bytes 1310720 | tf_op jit(solution)/shard_map/all_gather | solution.py:57
  12.4 61.2 %reduce-scatter.5.cloned.1.call-start = ((), (), s32[]{:S(2)}) async-start(), calls=%async_computation.3 | async-start | bytes 1310720 | tf_op jit(solution)/shard_map/reduce_scatter | solution.py:49
  41.9 4.1 %copy-start.1 = (s32[256]{0:T(256)S(1)}, s32[256]{0:T(256)}, u32[]{:S(2)}) copy-start(s32[256]{0:T(256)} %param.13) | copy-start | bytes 3076
Sparse Core Ops, SparseCore 0:
  11.9 14.3 reduce-scatter.2
Sparse Core Ops, SparseCore 1:
  13.8 30.5 all-gather.1
  46.7 26.9 reduce-scatter.4
where the time goes:
time: 92 us; the launch traced here: 91.8 us
  waiting for transfers between devices  28.1 us (31%)
  blocking collectives  27.1 us (29%)
  matrix products  15.8 us (17%)
  between operations  14.9 us (16%)
  other arithmetic  3.41 us (4%)
  local copies, waits for them, and re-layouts  2.46 us (3%)
    reduce_scatter x1, waiting for transfers between devices, per_device(): lax.psum_scatter(masked_product(step_starts, step_ends, positions, out_ro...  27.5 us
    psum x1, blocking collectives, per_device(): in_total = lax.psum(in_part, 'mp')  18.7 us
    psum x1, blocking collectives, per_device(): totals = lax.psum(partial_value, 'mp')  8.41 us
    dot_general x1, matrix products, per_device(): jnp.dot(activations, in_projection, preferred_element_type=jnp.float32)  7.23 us
    dot_general x1, matrix products, per_device(): jnp.dot(cotangent, out_projection, preferred_element_type=jnp.float32)  4.4 us
    dot_general x1, matrix products, masked_product(): jnp.dot(weighted.reshape(step_count * share_rows, positions.shape[0]), in...  2.39 us
  transfers between devices with their start and end apart: 3, of which 1 were waited for; matrix products, arithmetic and copies ran while one was open for 16% of the time, Pallas kernels for 0%

commit v1 on v0

v1 whole, which is shorter than its diff:
```python
import functools

import jax
import jax.numpy as jnp
from jax import lax
from jax.experimental import pallas as pl
from jax.experimental.pallas import tpu as pltpu
from jax.sharding import PartitionSpec as P

MESH = pl.DeviceIdType.MESH
CHUNK = 256
GROUP = 4


def nt(left, right):
    return lax.dot_general(
        left, right, (((1,), (1,)), ((), ())), preferred_element_type=jnp.float32
    )


def kernel(
    nseq, nmp, nb,
    hid_hbm, cot_hbm, win_hbm, wout_hbm, len_ref, q_hbm,
    out_ref,
    hid, cot, win, wout, qbuf, inbuf, outown, outrecv, gacc, sbuf, srecv,
    hid_sem, cot_sem, w_sem, qloc_sem,
    in_ssem, in_rsem, out_ssem, out_rsem, q_ssem, q_rsem, qb_ssem, qb_rsem, s_ssem, s_rsem,
):
    tokens = hid.shape[0]
    rank = win.shape[1]
    share = rank // nmp
    steps = len_ref.shape[1]
    chunks = tokens // CHUNK
    mine = steps // nseq
    z = lax.axis_index("seq")
    x = lax.axis_index("mp")
    b = lax.axis_index("batch")

    w_copies = [
        pltpu.make_async_copy(wout_hbm, wout, w_sem.at[0]),
        pltpu.make_async_copy(win_hbm, win, w_sem.at[1]),
    ]
    rows = lambda c: pl.ds(c * CHUNK, CHUNK)
    cot_copies = [
        pltpu.make_async_copy(cot_hbm.at[0, rows(c)], cot.at[rows(c)], cot_sem.at[c])
        for c in range(chunks)
    ]
    hid_copies = [
        pltpu.make_async_copy(hid_hbm.at[0, rows(c)], hid.at[rows(c)], hid_sem.at[c])
        for c in range(chunks)
    ]
    q_local = pltpu.make_async_copy(q_hbm, qbuf.at[z], qloc_sem)
    w_copies[0].start()
    for copy in cot_copies:
        copy.start()
    w_copies[1].start()
    hid_copies[0].start()
    q_local.start()
    for copy in hid_copies[1:]:
        copy.start()

    barrier = pltpu.get_barrier_semaphore()
    total = nseq * nmp
    flat = z * nmp + x

    def greet(d, carry):
        peer = lax.rem(flat + d, total)
        pl.semaphore_signal(
            barrier, inc=1, device_id={"seq": peer // nmp, "mp": lax.rem(peer, nmp)},
            device_id_type=MESH,
        )
        return carry

    lax.fori_loop(1, total, greet, 0)
    for d in range(1, nb):
        pl.semaphore_signal(
            barrier, inc=1, device_id={"batch": lax.rem(b + d, nb)}, device_id_type=MESH
        )
    pl.semaphore_wait(barrier, total - 1 + nb - 1)

    def q_copy(owner, peer):
        return pltpu.make_async_remote_copy(
            src_ref=q_hbm.at[b], dst_ref=qbuf.at[owner, b],
            send_sem=q_ssem.at[peer], recv_sem=q_rsem.at[owner],
            device_id={"seq": peer}, device_id_type=MESH,
        )

    def qb_copy(owner, core, peer):
        return pltpu.make_async_remote_copy(
            src_ref=qbuf.at[owner, core], dst_ref=qbuf.at[owner, core],
            send_sem=qb_ssem.at[owner, peer], recv_sem=qb_rsem.at[owner, core],
            device_id={"batch": peer}, device_id_type=MESH,
        )

    others_z = [lax.rem(z + d, nseq) for d in range(1, nseq)]
    others_x = [lax.rem(x + d, nmp) for d in range(1, nmp)]
    others_b = [lax.rem(b + d, nb) for d in range(1, nb)]
    for peer in others_z:
        q_copy(z, peer).start()

    def out_copy(owner, peer, c):
        return pltpu.make_async_remote_copy(
            src_ref=outown.at[c, peer], dst_ref=outrecv.at[c, owner],
            send_sem=out_ssem.at[c, peer], recv_sem=out_rsem.at[c, owner],
            device_id={"mp": peer}, device_id_type=MESH,
        )

    def in_copy(owner, peer, c):
        return pltpu.make_async_remote_copy(
            src_ref=inbuf.at[c, x], dst_ref=inbuf.at[c, owner],
            send_sem=in_ssem.at[c, peer], recv_sem=in_rsem.at[c, owner],
            device_id={"mp": peer}, device_id_type=MESH,
        )

    w_copies[0].wait()
    for c in range(chunks):
        cot_copies[c].wait()
        part = jnp.dot(cot[rows(c), :], wout[...], preferred_element_type=jnp.float32)
        outown[c] = part.T.reshape(nmp, share, CHUNK)
        for peer in others_x:
            out_copy(x, peer, c).start()
        outrecv[c, x] = outown[c, x]

    lengths = len_ref[...].astype(jnp.float32)
    row = lax.broadcasted_iota(jnp.int32, (steps, steps), 0)
    col = lax.broadcasted_iota(jnp.int32, (steps, steps), 1)
    spread = jnp.broadcast_to(lengths, (steps, steps))
    ends = jnp.sum(jnp.where(col <= row, spread, 0.0), axis=1, keepdims=True).astype(jnp.int32)
    starts = jnp.sum(jnp.where(col < row, spread, 0.0), axis=1, keepdims=True).astype(jnp.int32)

    def project(c):
        if c == 0:
            w_copies[1].wait()
        hid_copies[c].wait()
        part = jnp.dot(hid[rows(c), :], win[...], preferred_element_type=jnp.float32)
        inbuf[c, x] = part.T
        for peer in others_x:
            in_copy(x, peer, c).start()

    def gradients(c):
        for peer in others_x:
            out_copy(peer, peer, c).wait_recv()
            in_copy(peer, peer, c).wait_recv()
        out_total = outrecv[c, 0]
        in_total = inbuf[c, 0]
        for m in range(1, nmp):
            out_total = out_total + outrecv[c, m]
            in_total = in_total + inbuf[c, m]
        out_low = out_total.astype(jnp.bfloat16).astype(jnp.float32)
        in_low = in_total.astype(jnp.bfloat16)
        pos = (
            lax.broadcasted_iota(jnp.int32, (steps, CHUNK), 1) + (z * tokens + c * CHUNK)
        )
        member = jnp.where((pos >= starts) & (pos < ends), 1.0, 0.0).astype(jnp.bfloat16)
        member = member.reshape(steps // 16, 16, CHUNK)
        zero = jnp.zeros((rank, CHUNK), jnp.bfloat16)
        right = jnp.concatenate(
            [
                jnp.concatenate([in_low if i == k else zero for i in range(GROUP)], axis=1)
                for k in range(GROUP)
            ],
            axis=0,
        )
        width = GROUP * rank
        for g in range(share // GROUP):
            left = []
            for j in range(g * GROUP, (g + 1) * GROUP):
                line = jnp.broadcast_to(out_low[j:j + 1, :], (16, CHUNK)).astype(jnp.bfloat16)
                left.append((member * line[None]).reshape(steps, CHUNK))
            term = nt(jnp.concatenate(left, axis=1), right)
            at = pl.ds(g * width, width)
            if c == 0:
                gacc[:, at] = term
            else:
                gacc[:, at] += term

    project(0)
    for c in range(1, chunks):
        project(c)
        gradients(c - 1)

    for owner in others_z:
        q_copy(owner, owner).wait_recv()
        for peer in others_b:
            qb_copy(owner, b, peer).start()
    gradients(chunks - 1)
    low = gacc[...].astype(jnp.bfloat16)
    q_local.wait()
    for owner in others_z:
        for core in others_b:
            qb_copy(owner, core, core).wait_recv()
    queries = qbuf[...].reshape(nseq * nb * qbuf.shape[2], qbuf.shape[3])
    part = nt(low, queries).astype(jnp.bfloat16)
    sbuf[...] = part.reshape(nseq, mine, part.shape[1])
    srecv[flat] = sbuf[z]

    def s_copy(owner, peer):
        return pltpu.make_async_remote_copy(
            src_ref=sbuf.at[peer // nmp], dst_ref=srecv.at[owner],
            send_sem=s_ssem.at[peer], recv_sem=s_rsem.at[owner],
            device_id={"seq": peer // nmp, "mp": lax.rem(peer, nmp)}, device_id_type=MESH,
        )

    def s_start(d, carry):
        s_copy(flat, lax.rem(flat + d, total)).start()
        return carry

    def s_wait(d, carry):
        peer = lax.rem(flat + d, total)
        s_copy(peer, peer).wait_recv()
        return carry

    def s_done(d, carry):
        s_copy(flat, lax.rem(flat + d, total)).wait_send()
        return carry

    lax.fori_loop(1, total, s_start, 0)
    for peer in others_z:
        q_copy(z, peer).wait_send()
    for owner in others_z:
        for peer in others_b:
            qb_copy(owner, b, peer).wait_send()
    for c in range(chunks):
        for peer in others_x:
            out_copy(x, peer, c).wait_send()
            in_copy(x, peer, c).wait_send()
    lax.fori_loop(1, total, s_wait, 0)
    out_ref[...] = lax.fori_loop(
        1, total, lambda i, acc: acc + srecv[i].astype(jnp.float32),
        srecv[0].astype(jnp.float32),
    )
    lax.fori_loop(1, total, s_done, 0)


def per_device(
    nseq, nmp, nb,
    hidden_acts, out_cotangent, in_projection, out_projection, step_lengths, query_grads, query_trace,
):
    tokens, units = hidden_acts.shape[1:]
    features = out_cotangent.shape[2]
    rank = in_projection.shape[1]
    share = rank // nmp
    steps = step_lengths.shape[1]
    local, entries = query_grads.shape
    queries = local * nseq
    chunks = tokens // CHUNK
    mine = steps // nseq
    total = nseq * nmp
    any_spec = pl.BlockSpec(memory_space=pl.ANY)
    vmem_spec = pl.BlockSpec(memory_space=pltpu.VMEM)
    dma = pltpu.SemaphoreType.DMA
    totals = pl.pallas_call(
        functools.partial(kernel, nseq, nmp, nb),
        out_shape=jax.ShapeDtypeStruct((mine, queries), jnp.float32),
        in_specs=[any_spec, any_spec, any_spec, any_spec, vmem_spec, any_spec],
        out_specs=vmem_spec,
        scratch_shapes=[
            pltpu.VMEM((tokens, units), jnp.bfloat16),
            pltpu.VMEM((tokens, features), jnp.bfloat16),
            pltpu.VMEM((units, rank), jnp.bfloat16),
            pltpu.VMEM((features, rank), jnp.bfloat16),
            pltpu.VMEM((nseq, nb, local // nb, entries), jnp.bfloat16),
            pltpu.VMEM((chunks, nmp, rank, CHUNK), jnp.float32),
            pltpu.VMEM((chunks, nmp, share, CHUNK), jnp.float32),
            pltpu.VMEM((chunks, nmp, share, CHUNK), jnp.float32),
            pltpu.VMEM((steps, share * rank), jnp.float32),
            pltpu.VMEM((nseq, mine, queries), jnp.bfloat16),
            pltpu.VMEM((total, mine, queries), jnp.bfloat16),
            dma((chunks,)), dma((chunks,)), dma((2,)), dma,
            dma((chunks, nmp)), dma((chunks, nmp)), dma((chunks, nmp)), dma((chunks, nmp)),
            dma((nseq,)), dma((nseq,)), dma((nseq, nb)), dma((nseq, nb)),
            dma((total,)), dma((total,)),
        ],
        compiler_params=pltpu.CompilerParams(
            collective_id=0, has_side_effects=True, vmem_limit_bytes=56 * 1024 * 1024
        ),
        cost_estimate=pl.CostEstimate(
            flops=2 * tokens * (units + features) * rank + 2 * steps * share * tokens * rank,
            bytes_accessed=2 * tokens * (units + features), transcendentals=0,
        ),
        name="influence",
    )(
        hidden_acts, out_cotangent, in_projection, out_projection, step_lengths,
        query_grads.reshape(nb, local // nb, entries),
    )
    keep = query_trace[None, :] != lax.axis_index("batch")
    return jnp.where(keep, totals, jnp.zeros((), jnp.float32))[None]


def solution(mesh):
    return jax.shard_map(
        functools.partial(per_device, mesh.shape["seq"], mesh.shape["mp"], mesh.shape["batch"]),
        mesh=mesh,
        in_specs=(
            P(("parts", "batch"), "seq", "mp"),
            P(("parts", "batch"), "seq", "mp"),
            P("mp", None),
            P("mp", None),
            P(("parts", "batch"), None),
            P("seq", "mp"),
            P(),
        ),
        out_specs=P(("parts", "batch"), "seq", None),
        check_vma=False,
    )
```

time: 92 us -> 36.4 us (0.40)
  Pallas kernels: 0 us -> 30.2 us
  waiting for transfers between devices: 28.1 us -> 0 us
  blocking collectives: 27.1 us -> 0 us
  matrix products: 15.8 us -> 0 us
  between operations: 14.9 us -> 0.03 us
  local copies, waits for them, and re-layouts: 2.46 us -> 4.61 us
  other arithmetic: 3.41 us -> 1.38 us
    pallas_call x0 -> x1, Pallas kernels: none -> 30.2 us  [per_device(): pl.pallas_call(functools.partial(kernel, nseq, nmp, nb), out_shape=jax.Sh...]
    reduce_scatter x2 -> x0, waiting for transfers between devices: 27.5 us -> none  [the longest x1 27.5 us: per_device(): lax.psum_scatter(masked_product(step_starts, step_ends, positions, out_ro...]
    psum x2 -> x0, blocking collectives: 27.1 us -> none  [the longest x1 18.7 us: per_device(): in_total = lax.psum(in_part, 'mp')]
    dot_general x4 -> x0, matrix products: 15.8 us -> none  [the longest x1 7.23 us: per_device(): jnp.dot(activations, in_projection, preferred_element_type=jnp.float32)]
    unnamed x4, local copies, waits for them, and re-layouts: 0.01 us -> 4.61 us
    reshape x1 -> x0, local copies, waits for them, and re-layouts: 1.69 us -> none  [masked_product(): return gradients.reshape(step_count, share_rows * in_rows.shape[1])]
  transfers between devices with their start and end apart: 3 -> 0, of which waited for: 1 -> 0; matrix products, arithmetic and copies ran while one was open for 16% -> 0% of each run, Pallas kernels for 0% -> 0%
where the time goes in v1:
time: 36.4 us; the launch traced here: 36.2 us
  Pallas kernels  30.2 us (83%)
  local copies, waits for them, and re-layouts  4.61 us (13%)
  other arithmetic  1.38 us (4%)
    pallas_call x1, Pallas kernels, per_device(): pl.pallas_call(functools.partial(kernel, nseq, nmp, nb), out_shape=jax.Sh...  30.2 us
    unnamed x4, local copies, waits for them, and re-layouts  4.61 us
    broadcast_in_dim x1, other arithmetic, per_device(): return jnp.where(keep, totals, jnp.zeros((), jnp.float32))[None]  1.38 us

profile of v1, /device:TPU:0, one launch (start us, length us, event | category | flops | bytes accessed | tf_op | source)
XLA Modules:
  0.0 36.2 jit_solution(1400039167891346370)
XLA Ops:
  0.0 2.6 %copy.8.win_hbm = bf16[7168,64]{1,0:T(8,128)(2,1)} copy(bf16[7168,64]{0,1:T(8,128)(2,1)} %param.9) | data formatting | bytes 1835008 | tf_op args[2]
  2.6 2.0 %copy.9.wout_hbm = bf16[2048,64]{1,0:T(8,128)(2,1)} copy(bf16[2048,64]{0,1:T(8,128)(2,1)} %param.10) | data formatting | bytes 524288 | tf_op args[3]
  4.6 0.0 copy-start
  4.6 30.2 %influence.1 = f32[32,256]{1,0:T(8,128)} custom-call(bf16[1,1024,7168]{2,1,0:T(8,128)(2,1)} %hid_hbm.1, bf16[1,1024,2048]{2,1,0:T(8,128)(2,1)} %cot_hbm.1, bf16[7168,64]{1,0:T(8,128)(2,1)} %copy.8.win_hbm, bf16[2048,64]{1,0:T(8,128)(2,1)} %copy.9.wout_hbm, s32[1,128]{1,0:T(1,128)} %len_ref.1, bf16[2,32,2048]{2,1,0:T(8,128)(2,1)} %bitcast.3), custom_call_target="tpu_custom_call" | custom-call | flops 1744830464 | bytes 18874368 | tf_op jit(solution)/shard_map/influence/pallas_call | solution.py:252
  34.8 0.0 copy-done
  34.8 1.4 %select_bitcast_fusion = f32[1,32,256]{2,1,0:T(8,128)} fusion(f32[32,256]{1,0:T(8,128)} %influence.1, pred[256]{0:T(512)(128)(4,1)S(1)} %broadcast_compare_fusion), kind=kLoop, calls=%fused_computation | loop fusion | flops 8192 | bytes 65792 | tf_op jit(solution)/shard_map/broadcast_in_dim | solution.py:287
  (1 shorter events, 0.0 us)
Async XLA Ops:
  4.6 30.2 %copy-start = (s32[256]{0:T(256)S(1)}, s32[256]{0:T(256)}, u32[]{:S(2)}) copy-start(s32[256]{0:T(256)} %param.13) | copy-start | bytes 3076

commit v2 on v1

--- a/solution.py
+++ b/solution.py
@@ -10,6 +10,8 @@
 MESH = pl.DeviceIdType.MESH
 CHUNK = 256
 GROUP = 4
+DEPTH = 1
+LAG = 2
 
 
 def nt(left, right):
@@ -22,12 +24,12 @@
     nseq, nmp, nb,
     hid_hbm, cot_hbm, win_hbm, wout_hbm, len_ref, q_hbm,
     out_ref,
-    hid, cot, win, wout, qbuf, inbuf, outown, outrecv, gacc, sbuf, srecv,
+    hid, cot, win, wout, qbuf, inbuf, outown, outrecv, lhs, gacc, sbuf, srecv,
     hid_sem, cot_sem, w_sem, qloc_sem,
     in_ssem, in_rsem, out_ssem, out_rsem, q_ssem, q_rsem, qb_ssem, qb_rsem, s_ssem, s_rsem,
 ):
     tokens = hid.shape[0]
-    rank = win.shape[1]
+    rank = win.shape[0]
     share = rank // nmp
     steps = len_ref.shape[1]
     chunks = tokens // CHUNK
@@ -40,24 +42,21 @@
         pltpu.make_async_copy(wout_hbm, wout, w_sem.at[0]),
         pltpu.make_async_copy(win_hbm, win, w_sem.at[1]),
     ]
-    rows = lambda c: pl.ds(c * CHUNK, CHUNK)
-    cot_copies = [
-        pltpu.make_async_copy(cot_hbm.at[0, rows(c)], cot.at[rows(c)], cot_sem.at[c])
-        for c in range(chunks)
-    ]
-    hid_copies = [
-        pltpu.make_async_copy(hid_hbm.at[0, rows(c)], hid.at[rows(c)], hid_sem.at[c])
-        for c in range(chunks)
-    ]
+    rows = lambda c: pl.ds(pl.multiple_of(c * CHUNK, CHUNK), CHUNK)
+
+    def cot_copy(c):
+        return pltpu.make_async_copy(cot_hbm.at[0, rows(c)], cot.at[rows(c)], cot_sem.at[c])
+
+    def hid_copy(c):
+        return pltpu.make_async_copy(hid_hbm.at[0, rows(c)], hid.at[rows(c)], hid_sem.at[c])
+
     q_local = pltpu.make_async_copy(q_hbm, qbuf.at[z], qloc_sem)
     w_copies[0].start()
-    for copy in cot_copies:
-        copy.start()
+    for c in range(chunks):
+        cot_copy(c).start()
     w_copies[1].start()
-    hid_copies[0].start()
-    q_local.start()
-    for copy in hid_copies[1:]:
-        copy.start()
+    for c in range(min(DEPTH, chunks)):
+        hid_copy(c).start()
 
     barrier = pltpu.get_barrier_semaphore()
     total = nseq * nmp
@@ -113,13 +112,17 @@
         )
 
     w_copies[0].wait()
-    for c in range(chunks):
-        cot_copies[c].wait()
-        part = jnp.dot(cot[rows(c), :], wout[...], preferred_element_type=jnp.float32)
+
+    def features_step(c, carry):
+        cot_copy(c).wait()
+        part = nt(cot[rows(c), :], wout[...])
         outown[c] = part.T.reshape(nmp, share, CHUNK)
         for peer in others_x:
             out_copy(x, peer, c).start()
         outrecv[c, x] = outown[c, x]
+        return carry
+
+    lax.fori_loop(0, chunks, features_step, 0)
 
     lengths = len_ref[...].astype(jnp.float32)
     row = lax.broadcasted_iota(jnp.int32, (steps, steps), 0)
@@ -129,10 +132,13 @@
     starts = jnp.sum(jnp.where(col < row, spread, 0.0), axis=1, keepdims=True).astype(jnp.int32)
 
     def project(c):
-        if c == 0:
-            w_copies[1].wait()
-        hid_copies[c].wait()
-        part = jnp.dot(hid[rows(c), :], win[...], preferred_element_type=jnp.float32)
+        hid_copy(c).wait()
+
+        @pl.when(c < chunks - DEPTH)
+        def _():
+            hid_copy(c + DEPTH).start()
+
+        part = nt(hid[rows(c), :], win[...])
         inbuf[c, x] = part.T
         for peer in others_x:
             in_copy(x, peer, c).start()
@@ -161,30 +167,38 @@
             ],
             axis=0,
         )
-        width = GROUP * rank
-        for g in range(share // GROUP):
-            left = []
-            for j in range(g * GROUP, (g + 1) * GROUP):
-                line = jnp.broadcast_to(out_low[j:j + 1, :], (16, CHUNK)).astype(jnp.bfloat16)
-                left.append((member * line[None]).reshape(steps, CHUNK))
-            term = nt(jnp.concatenate(left, axis=1), right)
-            at = pl.ds(g * width, width)
-            if c == 0:
-                gacc[:, at] = term
-            else:
-                gacc[:, at] += term
-
-    project(0)
-    for c in range(1, chunks):
-        project(c)
-        gradients(c - 1)
+        for j in range(share):
+            line = jnp.broadcast_to(out_low[j:j + 1, :], (16, CHUNK)).astype(jnp.bfloat16)
+            lhs[
+                pl.ds(j // GROUP * steps, steps), pl.ds(j % GROUP * CHUNK, CHUNK)
+            ] = (member * line[None]).reshape(steps, CHUNK)
+        gacc[...] += nt(lhs[...], right)
+
+    gacc[...] = jnp.zeros_like(gacc)
+    w_copies[1].wait()
+
+    def hidden_step(c, carry):
+        @pl.when(c < chunks)
+        def _():
+            project(c)
+
+        @pl.when(c >= LAG)
+        def _():
+            gradients(c - LAG)
+
+        return carry
+
+    q_local.start()
+    lax.fori_loop(0, chunks + LAG, hidden_step, 0)
 
     for owner in others_z:
         q_copy(owner, owner).wait_recv()
         for peer in others_b:
             qb_copy(owner, b, peer).start()
-    gradients(chunks - 1)
-    low = gacc[...].astype(jnp.bfloat16)
+    low = jnp.concatenate(
+        [gacc[pl.ds(g * steps, steps), :].astype(jnp.bfloat16) for g in range(share // GROUP)],
+        axis=1,
+    )
     q_local.wait()
     for owner in others_z:
         for core in others_b:
@@ -257,13 +271,14 @@
         scratch_shapes=[
             pltpu.VMEM((tokens, units), jnp.bfloat16),
             pltpu.VMEM((tokens, features), jnp.bfloat16),
-            pltpu.VMEM((units, rank), jnp.bfloat16),
-            pltpu.VMEM((features, rank), jnp.bfloat16),
+            pltpu.VMEM((rank, units), jnp.bfloat16),
+            pltpu.VMEM((rank, features), jnp.bfloat16),
             pltpu.VMEM((nseq, nb, local // nb, entries), jnp.bfloat16),
             pltpu.VMEM((chunks, nmp, rank, CHUNK), jnp.float32),
             pltpu.VMEM((chunks, nmp, share, CHUNK), jnp.float32),
             pltpu.VMEM((chunks, nmp, share, CHUNK), jnp.float32),
-            pltpu.VMEM((steps, share * rank), jnp.float32),
+            pltpu.VMEM((share // GROUP * steps, GROUP * CHUNK), jnp.bfloat16),
+            pltpu.VMEM((share // GROUP * steps, GROUP * rank), jnp.float32),
             pltpu.VMEM((nseq, mine, queries), jnp.bfloat16),
             pltpu.VMEM((total, mine, queries), jnp.bfloat16),
             dma((chunks,)), dma((chunks,)), dma((2,)), dma,
@@ -280,7 +295,7 @@
         ),
         name="influence",
     )(
-        hidden_acts, out_cotangent, in_projection, out_projection, step_lengths,
+        hidden_acts, out_cotangent, in_projection.T, out_projection.T, step_lengths,
         query_grads.reshape(nb, local // nb, entries),
     )
     keep = query_trace[None, :] != lax.axis_index("batch")

time: 36.4 us -> 28.6 us (0.79)
  the two profiles are of different devices: /device:TPU:0 before, /device:TPU:1 now
where the time goes in v2:
time: 28.6 us; the launch traced here: 28.3 us
  Pallas kernels  26.3 us (92%)
  other arithmetic  2.06 us (7%)
    pallas_call x1, Pallas kernels, per_device(): pl.pallas_call(functools.partial(kernel, nseq, nmp, nb), out_shape=jax.Sh...  26.3 us
    broadcast_in_dim x1, other arithmetic, per_device(): return jnp.where(keep, totals, jnp.zeros((), jnp.float32))[None]  1.38 us
    ne x1, other arithmetic, per_device(): keep = query_trace[None, :] != lax.axis_index('batch')  0.68 us

profile of v2, /device:TPU:1, one launch (start us, length us, event | category | flops | bytes accessed | tf_op | source)
XLA Modules:
  0.0 28.3 jit_solution(10964047806809989691)
XLA Ops:
  0.0 0.7 %broadcast_compare_fusion = pred[256]{0:T(512)(128)(4,1)S(1)} fusion(s32[256]{0:T(256)} %param.13, s32[]{:T(128)S(6)} %axis_index.12), kind=kLoop, calls=%fused_computation.1 | loop fusion | flops 256 | bytes 1284 | tf_op jit(solution)/shard_map/ne | solution.py:301
  0.7 26.3 %influence.1 = f32[32,256]{1,0:T(8,128)} custom-call(bf16[1,1024,7168]{2,1,0:T(8,128)(2,1)} %hid_hbm.1, bf16[1,1024,2048]{2,1,0:T(8,128)(2,1)} %cot_hbm.1, bf16[64,7168]{1,0:T(8,128)(2,1)} %bitcast.5, bf16[64,2048]{1,0:T(8,128)(2,1)} %bitcast.6, s32[1,128]{1,0:T(1,128)} %len_ref.1, bf16[2,32,2048]{2,1,0:T(8,128)(2,1)} %bitcast.7), custom_call_target="tpu_custom_call" | custom-call | flops 1744830464 | bytes 18874368 | tf_op jit(solution)/shard_map/influence/pallas_call | solution.py:266
  26.9 1.4 %select_bitcast_fusion = f32[1,32,256]{2,1,0:T(8,128)} fusion(f32[32,256]{1,0:T(8,128)} %influence.1, pred[256]{0:T(512)(128)(4,1)S(1)} %broadcast_compare_fusion), kind=kLoop, calls=%fused_computation | loop fusion | flops 8192 | bytes 65792 | tf_op jit(solution)/shard_map/broadcast_in_dim | solution.py:302

commit v3 on v2

--- a/solution.py
+++ b/solution.py
@@ -10,7 +10,7 @@
 MESH = pl.DeviceIdType.MESH
 CHUNK = 256
 GROUP = 4
-DEPTH = 1
+DEPTH = 2
 LAG = 2
 
 
@@ -22,7 +22,7 @@
 
 def kernel(
     nseq, nmp, nb,
-    hid_hbm, cot_hbm, win_hbm, wout_hbm, len_ref, q_hbm,
+    hid_hbm, cot_hbm, win_hbm, wout_hbm, len_ref, q_hbm, trace_ref,
     out_ref,
     hid, cot, win, wout, qbuf, inbuf, outown, outrecv, lhs, gacc, sbuf, srecv,
     hid_sem, cot_sem, w_sem, qloc_sem,
@@ -182,6 +182,13 @@
         def _():
             project(c)
 
+        @pl.when(c == chunks + LAG - 1)
+        def _():
+            for owner in others_z:
+                q_copy(owner, owner).wait_recv()
+                for peer in others_b:
+                    qb_copy(owner, b, peer).start()
+
         @pl.when(c >= LAG)
         def _():
             gradients(c - LAG)
@@ -191,10 +198,6 @@
     q_local.start()
     lax.fori_loop(0, chunks + LAG, hidden_step, 0)
 
-    for owner in others_z:
-        q_copy(owner, owner).wait_recv()
-        for peer in others_b:
-            qb_copy(owner, b, peer).start()
     low = jnp.concatenate(
         [gacc[pl.ds(g * steps, steps), :].astype(jnp.bfloat16) for g in range(share // GROUP)],
         axis=1,
@@ -239,10 +242,11 @@
             out_copy(x, peer, c).wait_send()
             in_copy(x, peer, c).wait_send()
     lax.fori_loop(1, total, s_wait, 0)
-    out_ref[...] = lax.fori_loop(
+    score = lax.fori_loop(
         1, total, lambda i, acc: acc + srecv[i].astype(jnp.float32),
         srecv[0].astype(jnp.float32),
     )
+    out_ref[0] = jnp.where(trace_ref[...] != b, score, 0.0)
     lax.fori_loop(1, total, s_done, 0)
 
 
@@ -263,10 +267,10 @@
     any_spec = pl.BlockSpec(memory_space=pl.ANY)
     vmem_spec = pl.BlockSpec(memory_space=pltpu.VMEM)
     dma = pltpu.SemaphoreType.DMA
-    totals = pl.pallas_call(
+    return pl.pallas_call(
         functools.partial(kernel, nseq, nmp, nb),
-        out_shape=jax.ShapeDtypeStruct((mine, queries), jnp.float32),
-        in_specs=[any_spec, any_spec, any_spec, any_spec, vmem_spec, any_spec],
+        out_shape=jax.ShapeDtypeStruct((1, mine, queries), jnp.float32),
+        in_specs=[any_spec, any_spec, any_spec, any_spec, vmem_spec, any_spec, vmem_spec],
         out_specs=vmem_spec,
         scratch_shapes=[
             pltpu.VMEM((tokens, units), jnp.bfloat16),
@@ -296,10 +300,8 @@
         name="influence",
     )(
         hidden_acts, out_cotangent, in_projection.T, out_projection.T, step_lengths,
-        query_grads.reshape(nb, local // nb, entries),
-    )
-    keep = query_trace[None, :] != lax.axis_index("batch")
-    return jnp.where(keep, totals, jnp.zeros((), jnp.float32))[None]
+        query_grads.reshape(nb, local // nb, entries), query_trace[None],
+    )
 
 
 def solution(mesh):

time: 28.6 us -> 27.6 us (0.965)
  the two profiles are of different devices: /device:TPU:1 before, /device:TPU:0 now
where the time goes in v3:
time: 27.6 us; the launch traced here: 27.4 us
  Pallas kernels  26 us (94%)
  local copies, waits for them, and re-layouts  1.38 us (5%)
    pallas_call x1, Pallas kernels, per_device(): pl.pallas_call(functools.partial(kernel, nseq, nmp, nb), out_shape=jax.Sh...  26 us
    unnamed x1, local copies, waits for them, and re-layouts  1.38 us

profile of v3, /device:TPU:0, one launch (start us, length us, event | category | flops | bytes accessed | tf_op | source)
XLA Modules:
  0.0 27.4 jit_solution(2626910864913006161)
XLA Ops:
  0.0 26.0 %influence.1 = f32[1,32,256]{2,1,0:T(8,128)} custom-call(bf16[1,1024,7168]{2,1,0:T(8,128)(2,1)} %hid_hbm.1, bf16[1,1024,2048]{2,1,0:T(8,128)(2,1)} %cot_hbm.1, bf16[64,7168]{1,0:T(8,128)(2,1)} %bitcast.4, bf16[64,2048]{1,0:T(8,128)(2,1)} %bitcast.5, s32[1,128]{1,0:T(1,128)} %len_ref.1, bf16[2,32,2048]{2,1,0:T(8,128)(2,1)} %bitcast.6, s32[1,256]{1,0:T(1,128)} %bitcast.7), custom_call_target="tpu_custom_call" | custom-call | flops 1744830464 | bytes 18874368 | tf_op jit(solution)/shard_map/influence/pallas_call | solution.py:270
  26.0 1.4 %copy.9 = f32[1,32,256]{2,1,0:T(8,128)} copy(f32[1,32,256]{2,1,0:T(8,128)} %influence.1) | data formatting | bytes 65536
